TPU v7x, 32 devices: a whole 2x2x4 slice. The times are simulated.
32 devices in a mesh: seq: 8 (over z, y), head: 4 (over x, core).
Axes of the slice: x: 2, y: 2, z: 4, core: 2. Of those that a mesh axis runs over, the one named last changes fastest.
Arguments:
- query: bfloat16 [1024, 64, 576], P('seq', 'head'), may hold values from -10 to 10
- cache: bfloat16 [4096, 576], P('seq'), may hold values from -6 to 6
- grad_out: bfloat16 [1024, 64, 128], P('seq', 'head'), may hold values from -6 to 6
- value_weight: bfloat16 [64, 512, 128], P('head'), may hold values from -0.25 to 0.25
- picked: int32 [32, 4], P('seq'), may hold values from 0 to 31, as said below
Outputs:
- d_query: bfloat16 [1024, 64, 576], P('seq', 'head')
- d_cache: float32 [32, 128, 576], P('seq', 'head')
- d_value_weight: bfloat16 [64, 512, 128], P('head')
Inputs may be any that keep to these rules, and one draw needn't show every extreme that they name: `picked`: row g names 4 different blocks, each starting at or before the first query of block g. One of them is the block that holds query block g; every other one ends before position 3072. The rows of one index of seq together name at most 2 different blocks of any one owner (owner o holds blocks o * 4 to o * 4 + 3), and in every draw some owner has exactly 2 of its blocks named by every index of seq.
All inputs are finite; a program needn't handle non-finite values.
Results may differ from a plain program's by a relative error of at most 0.01.
Values may be sent and summed in bfloat16 or wider, within the bound.
A program may use at most 128 MiB of HBM per device.

v0:
```python
import jax
import jax.numpy as jnp
from jax import lax
from jax.sharding import PartitionSpec as P

KVL = 512
BLOCK = 128
QB = 32
TOPB = 4


SCORE_SCALE = 0.07216878364870323
MASKED = -1e30


def block_backward(q_rows, key_rows, d_latent, visible):
    value_rows = key_rows[:, :KVL]
    scores = (
        lax.dot_general(
            q_rows, key_rows, (((1,), (1,)), ((), ())), preferred_element_type=jnp.float32
        )
        * SCORE_SCALE
    )
    scores = jnp.where(visible, scores, MASKED)
    row_max = jnp.max(scores, axis=1, keepdims=True)
    exp_scores = jnp.exp(scores - row_max)
    weights = exp_scores / jnp.sum(exp_scores, axis=1, keepdims=True)
    weights_low = weights.astype(jnp.bfloat16)
    latent_out = jnp.dot(weights_low, value_rows, preferred_element_type=jnp.float32).astype(
        jnp.bfloat16
    )
    row_delta = jnp.sum(
        d_latent.astype(jnp.float32) * latent_out.astype(jnp.float32), axis=1, keepdims=True
    )
    d_probs = lax.dot_general(
        d_latent, value_rows, (((1,), (1,)), ((), ())), preferred_element_type=jnp.float32
    )
    d_scores = (SCORE_SCALE * weights * (d_probs - row_delta)).astype(jnp.bfloat16)
    d_query = jnp.dot(d_scores, key_rows, preferred_element_type=jnp.float32).astype(jnp.bfloat16)
    d_keys = lax.dot_general(
        d_scores, q_rows, (((0,), (0,)), ((), ())), preferred_element_type=jnp.float32
    )
    d_values = lax.dot_general(
        weights_low, d_latent, (((0,), (0,)), ((), ())), preferred_element_type=jnp.float32
    )
    d_keys = jnp.concatenate([d_keys[:, :KVL] + d_values, d_keys[:, KVL:]], axis=1)
    return (d_query, d_keys, latent_out)


def local(query, cache, grad_out, value_weight, picked):
    q_dev, heads_here, row_width = query.shape
    ctx_dev = cache.shape[0]
    owners = lax.axis_size("seq")
    seq_index = lax.axis_index("seq")
    quarters = lax.axis_size("head")
    quarter = lax.axis_index("head")
    block_count = ctx_dev // BLOCK
    qblocks_here = q_dev // QB
    entries = qblocks_here * TOPB
    capacity = max(q_dev // BLOCK, entries // owners)
    slot_total = owners * capacity
    sub_rows = BLOCK // quarters
    row_count = QB * heads_here
    flat_pick = picked.reshape(entries)
    owner_of = flat_pick // block_count
    global_ids = jnp.arange(owners * block_count, dtype=jnp.int32)
    matches = flat_pick[:, None] == global_ids[None, :]
    wanted = jnp.any(matches, axis=0).astype(jnp.int32).reshape(owners, block_count)
    order_in = jnp.cumsum(wanted, axis=1) - 1
    slot_ids = jnp.arange(capacity, dtype=jnp.int32)
    local_ids = jnp.arange(block_count, dtype=jnp.int32)
    holding = (wanted[:, None, :] == 1) & (order_in[:, None, :] == slot_ids[None, :, None])
    present = jnp.any(holding, axis=2)
    request = jnp.where(
        present, jnp.sum(jnp.where(holding, local_ids[None, None, :], 0), axis=2), -1
    )
    entry_rank = jnp.sum(
        jnp.where(matches, order_in.reshape(owners * block_count)[None, :], 0), axis=1
    )
    entry_slot = owner_of * capacity + entry_rank
    slot_map = (jnp.arange(slot_total, dtype=jnp.int32)[:, None] == entry_slot[None, :]).astype(
        jnp.float32
    )
    asked_rows = lax.all_to_all(request, "seq", split_axis=0, concat_axis=0, tiled=True).reshape(
        slot_total
    )
    owner_map = (local_ids[:, None] == asked_rows[None, :]).astype(jnp.float32)
    is_valid = asked_rows >= 0
    safe_ids = jnp.maximum(asked_rows, 0)
    cache_blocks = cache.reshape(block_count, BLOCK, row_width)
    part_blocks = lax.dynamic_slice_in_dim(cache_blocks, quarter * sub_rows, sub_rows, 1)
    packed = jnp.where(is_valid[:, None, None], jnp.take(part_blocks, safe_ids, axis=0), 0)
    fetched = lax.all_to_all(
        packed.reshape(owners, capacity, sub_rows, row_width),
        "seq",
        split_axis=0,
        concat_axis=0,
        tiled=True,
    )
    part_keys = jnp.take(fetched.reshape(slot_total, sub_rows, row_width), entry_slot, axis=0)
    entry_keys = lax.all_gather(part_keys, "head", axis=1, tiled=True)
    d_latent = jnp.einsum(
        "qhv,hcv->qhc", grad_out, value_weight, preferred_element_type=jnp.float32
    ).astype(jnp.bfloat16)
    first_pos = ctx_dev * owners - q_dev * owners + seq_index * q_dev

    def one_block(inputs):
        q_rows, latent_rows, key_rows, chosen, block_index = inputs
        query_pos = first_pos + block_index * QB + jnp.arange(QB, dtype=jnp.int32)
        row_pos = jnp.repeat(query_pos, heads_here)
        key_pos = (chosen[:, None] * BLOCK + jnp.arange(BLOCK, dtype=jnp.int32)[None, :]).reshape(
            TOPB * BLOCK
        )
        visible = key_pos[None, :] <= row_pos[:, None]
        return block_backward(q_rows, key_rows, latent_rows, visible)

    inputs = (
        query.reshape(qblocks_here, row_count, row_width),
        d_latent.reshape(qblocks_here, row_count, KVL),
        entry_keys.reshape(qblocks_here, TOPB * BLOCK, row_width),
        picked,
        jnp.arange(qblocks_here, dtype=jnp.int32),
    )
    d_query, d_keys, latent_out = lax.map(one_block, inputs)
    weight_terms = jnp.einsum(
        "qhc,qhv->hcv",
        latent_out.reshape(q_dev, heads_here, KVL),
        grad_out,
        preferred_element_type=jnp.float32,
    )
    d_value_weight = lax.psum(weight_terms, "seq").astype(jnp.bfloat16)
    entry_grads = d_keys.reshape(entries, BLOCK, row_width)
    shares = lax.psum_scatter(entry_grads, "head", scatter_dimension=1, tiled=True)
    slot_grads = jnp.dot(
        slot_map, shares.reshape(entries, sub_rows * row_width), precision=lax.Precision.HIGHEST
    )
    returned = lax.all_to_all(
        slot_grads.reshape(owners, capacity, sub_rows, row_width),
        "seq",
        split_axis=0,
        concat_axis=0,
        tiled=True,
    )
    d_cache = jnp.dot(
        owner_map,
        returned.reshape(slot_total, sub_rows * row_width),
        precision=lax.Precision.HIGHEST,
    ).reshape(block_count, sub_rows, row_width)
    return (d_query.reshape(q_dev, heads_here, row_width), d_cache, d_value_weight)


def solution(mesh):
    in_specs = (
        P("seq", "head", None),
        P("seq", None),
        P("seq", "head", None),
        P("head", None, None),
        P("seq", None),
    )
    out_specs = (P("seq", "head", None), P("seq", "head", None), P("head", None, None))
    return jax.shard_map(local, mesh=mesh, in_specs=in_specs, out_specs=out_specs, check_vma=False)
```

profile of v0, /device:TPU:0, one launch (start us, length us, event | category | flops | bytes accessed | tf_op | source)
XLA Modules:
  0.0 489.5 jit_solution(18433984785714928020)
XLA Ops:
  9.4 7.3 %all-to-all-start = ((s32[8,1,2]{2,1,0:T(1,128)}), s32[8,1,2]{2,1,0:T(1,128)S(1)}, u32[]{:S(2)}, u32[]{:S(2)}) async-start(s32[8,1,2]{2,1,0:T(1,128)} %copy.110), calls=%async_computation | async-start | bytes 8192 | tf_op jit(solution)/shard_map/all_to_all | solution.py:84
  18.1 5.0 %all-to-all-done = s32[8,1,2]{2,1,0:T(1,128)S(1)} async-done(((s32[8,1,2]{2,1,0:T(1,128)}), s32[8,1,2]{2,1,0:T(1,128)S(1)}, u32[]{:S(2)}, u32[]{:S(2)}) %all-to-all-start) | async-done | bytes 96 | tf_op jit(solution)/shard_map/all_to_all | solution.py:84
  25.2 3.5 all-to-all-start.1
  29.2 15.6 %all-to-all-done.1 = bf16[8,2,32,576]{3,2,1,0:T(8,128)(2,1)S(1)} async-done(((bf16[8,2,32,576]{3,2,1,0:T(8,128)(2,1)}), bf16[8,2,32,576]{3,2,1,0:T(8,128)(2,1)S(1)}, u32[]{:S(2)}, u32[]{:S(2)}) %all-to-all-start.1) | async-done | bytes 589856 | tf_op jit(solution)/shard_map/all_to_all | solution.py:93
  47.4 2.5 copy.118
  49.8 5.0 %copy.107 = bf16[128,16,576]{2,1,0:T(8,128)(2,1)} copy(bf16[128,16,576]{0,2,1:T(8,128)(2,1)} %param.7) | data formatting | bytes 4718592 | tf_op args[0]
  54.9 16.4 %all-gather.2.cloned.1.call-done = bf16[16,128,576]{2,1,0:T(8,128)(2,1)} async-done(((bf16[16,32,576]{2,1,0:T(8,128)(2,1)}), bf16[16,128,576]{2,1,0:T(8,128)(2,1)}) %all-gather.2.cloned.1.call-update) | async-done | bytes 2359312 | tf_op jit(solution)/shard_map/all_gather | solution.py:101
  71.3 150.0 %while.14 = (s32[]{:T(128)}, bf16[4,512,576]{1,2,0:T(8,128)(2,1)}, f32[4,512,576]{1,0,2:T(4,128)}, bf16[4,512,512]{2,1,0:T(8,128)(2,1)}, s32[4,4]{1,0:T(4,128)S(...) while((s32[]{:T(128)}, bf16[4,512,576]{1,2,0:T(8,128)(2,1)}, ...), condition=%wide.region_9.10_spmd, body=%wide.region_5.9_spmd.sunk | while | flops 1718156288 | bytes 29200884 | solution.py:124
  75.3 1.9 fusion.68
  78.7 1.6 fusion.72
  83.0 2.4 fusion.71
  85.5 23.4 %dynamic_update_slice.19 = f32[4,512,576]{1,0,2:T(4,128)} dynamic-update-slice(f32[4,512,576]{1,0,2:T(4,128)} %get-tuple-element.240, f32[1,512,576]{1,0,2:T(1,128)S(1)} %copy.155, s32[]{:T(128)S(6)} %copy.164, s32[]{:T(128)} %constant.93.clone.1..sunk, s32[]{:T(128)} %constant.93.clone.1..sunk) | dynamic-update-slice | bytes 2359300 | tf_op jit(solution)/shard_map/while/body/jit(dynamic_update_index_in_dim)/dynamic_update_slice | solution.py:124
  112.8 1.9 fusion.68
  120.5 2.4 fusion.71
  123.0 23.4 %dynamic_update_slice.19 = f32[4,512,576]{1,0,2:T(4,128)} dynamic-update-slice(f32[4,512,576]{1,0,2:T(4,128)} %get-tuple-element.240, f32[1,512,576]{1,0,2:T(1,128)S(1)} %copy.155, s32[]{:T(128)S(6)} %copy.164, s32[]{:T(128)} %constant.93.clone.1..sunk, s32[]{:T(128)} %constant.93.clone.1..sunk) | dynamic-update-slice | bytes 2359300 | tf_op jit(solution)/shard_map/while/body/jit(dynamic_update_index_in_dim)/dynamic_update_slice | solution.py:124
  150.4 1.9 fusion.68
  153.7 1.6 fusion.72
  158.0 2.4 fusion.71
  160.5 23.4 %dynamic_update_slice.19 = f32[4,512,576]{1,0,2:T(4,128)} dynamic-update-slice(f32[4,512,576]{1,0,2:T(4,128)} %get-tuple-element.240, f32[1,512,576]{1,0,2:T(1,128)S(1)} %copy.155, s32[]{:T(128)S(6)} %copy.164, s32[]{:T(128)} %constant.93.clone.1..sunk, s32[]{:T(128)} %constant.93.clone.1..sunk) | dynamic-update-slice | bytes 2359300 | tf_op jit(solution)/shard_map/while/body/jit(dynamic_update_index_in_dim)/dynamic_update_slice | solution.py:124
  187.9 1.9 fusion.68
  195.6 2.4 fusion.71
  198.0 23.4 %dynamic_update_slice.19 = f32[4,512,576]{1,0,2:T(4,128)} dynamic-update-slice(f32[4,512,576]{1,0,2:T(4,128)} %get-tuple-element.240, f32[1,512,576]{1,0,2:T(1,128)S(1)} %copy.155, s32[]{:T(128)S(6)} %copy.164, s32[]{:T(128)} %constant.93.clone.1..sunk, s32[]{:T(128)} %constant.93.clone.1..sunk) | dynamic-update-slice | bytes 2359300 | tf_op jit(solution)/shard_map/while/body/jit(dynamic_update_index_in_dim)/dynamic_update_slice | solution.py:124
  221.3 6.5 %reshape.314 = f32[16,128,576]{1,0,2:T(8,128)} reshape(f32[4,512,576]{1,0,2:T(4,128)} %get-tuple-element.58) | data formatting | bytes 9437184 | tf_op jit(solution)/shard_map/reshape | solution.py:132
  227.8 6.3 %copy.122 = f32[16,128,576]{2,0,1:T(8,128)} copy(f32[16,128,576]{1,0,2:T(8,128)} %reshape.314) | data formatting | bytes 9437184 | tf_op jit(solution)/shard_map/reshape | solution.py:132
  235.8 4.7 fusion.23
  240.5 4.4 copy.120
  244.9 4.7 copy.130
  249.7 36.1 %reduce-scatter.2.cloned.1.call-done = f32[16,32,576]{2,0,1:T(8,128)} async-done(((f32[16,128,576]{2,0,1:T(8,128)}), f32[16,32,576]{2,0,1:T(8,128)}) %reduce-scatter.2.cloned.1.call-update) | async-done | bytes 1179664 | tf_op jit(solution)/shard_map/reduce_scatter | solution.py:133
  285.7 1.7 copy.123
  291.6 5.5 %all-to-all-start.2 = ((f32[8,2,32,576]{3,2,1,0:T(8,128)}), f32[8,2,32,576]{3,2,1,0:T(8,128)S(1)}, u32[]{:S(2)}, u32[]{:S(2)}) async-start(f32[8,2,32,576]{3,2,1,0:T(8,128)} %copy.125), calls=%async_computation.3 | async-start | bytes 2621440 | tf_op jit(solution)/shard_map/all_to_all | solution.py:137
  297.1 179.8 %all-reduce.1 = bf16[16,512,128]{2,1,0:T(8,128)(2,1)} all-reduce(f32[16,512,128]{2,1,0:T(8,128)} %fusion.23), channel_id=1, replica_groups=mesh['seq'=8,'head'=4] {'seq'}, use_global_device_ids=true, to_apply=%region_11.12 | all-reduce | flops 1048576 | bytes 6291456 | tf_op jit(solution)/shard_map/psum | solution.py:131
  478.5 2.1 dot_general.43
  (140 shorter events, 50.9 us)
Async XLA Ops:
  7.2 39.5 %copy-start = (bf16[16,512,128]{2,1,0:T(8,128)(2,1)S(1)}, bf16[16,512,128]{2,1,0:T(8,128)(2,1)}, u32[]{:S(2)}) copy-start(bf16[16,512,128]{2,1,0:T(8,128)(2,1)} %param.10) | copy-start | bytes 6291460
  9.4 13.7 %all-to-all-start = ((s32[8,1,2]{2,1,0:T(1,128)}), s32[8,1,2]{2,1,0:T(1,128)S(1)}, u32[]{:S(2)}, u32[]{:S(2)}) async-start(s32[8,1,2]{2,1,0:T(1,128)} %copy.110), calls=%async_computation | async-start | bytes 8192 | tf_op jit(solution)/shard_map/all_to_all | solution.py:84
  18.0 10.8 %copy-start.5 = (s32[4,4]{1,0:T(4,128)S(1)}, s32[4,4]{1,0:T(4,128)}, u32[]{:S(2)}) copy-start(s32[4,4]{1,0:T(4,128)} %param.11) | copy-start | bytes 196
  25.2 19.7 %all-to-all-start.1 = ((bf16[8,2,32,576]{3,2,1,0:T(8,128)(2,1)}), bf16[8,2,32,576]{3,2,1,0:T(8,128)(2,1)S(1)}, u32[]{:S(2)}, u32[]{:S(2)}) async-start(bf16[8,2,32,576]{3,2,1,0:T(8,128)(2,1)} %select_select_fusion), calls=%async_computation.1 | async-start | bytes 1310720 | tf_op jit(solution)/shard_map/all_to_all | solution.py:93
  28.7 42.6 %all-gather.2.cloned.1.call-start = ((), (), s32[]{:S(2)}) async-start(), calls=%async_computation.4 | async-start | bytes 3276800 | tf_op jit(solution)/shard_map/all_gather | solution.py:101
  45.5 1.1 copy-start.3
  46.5 239.2 %reduce-scatter.2.cloned.1.call-start = ((), (), s32[]{:S(2)}) async-start(), calls=%async_computation.5 | async-start | bytes 6553600 | tf_op jit(solution)/shard_map/reduce_scatter | solution.py:133
  234.2 1.6 copy-start.2
  234.2 1.7 copy-start.4
  291.6 185.4 %all-to-all-start.2 = ((f32[8,2,32,576]{3,2,1,0:T(8,128)}), f32[8,2,32,576]{3,2,1,0:T(8,128)S(1)}, u32[]{:S(2)}, u32[]{:S(2)}) async-start(f32[8,2,32,576]{3,2,1,0:T(8,128)} %copy.125), calls=%async_computation.3 | async-start | bytes 2621440 | tf_op jit(solution)/shard_map/all_to_all | solution.py:137
  478.5 4.1 copy-start.1
Sparse Core Ops, SparseCore 0:
  46.7 24.5 all-gather.1
  234.3 51.3 reduce-scatter.1
where the time goes:
time: 494 us; the launch traced here: 489 us
  blocking collectives  180 us (36%)
  local copies, waits for them, and re-layouts  160 us (32%)
  waiting for transfers between devices  73.2 us (15%)
  matrix products  38.2 us (8%)
  starting transfers between devices  16.4 us (3%)
  between operations  14.3 us (3%)
  other arithmetic  4.99 us (1%)
    psum x1, blocking collectives, local(): d_value_weight = lax.psum(weight_terms, 'seq').astype(jnp.bfloat16)  180 us
    dynamic_update_slice x16, local copies, waits for them, and re-layouts, local(): d_query, d_keys, latent_out = lax.map(one_block, inputs)  102 us
    reduce_scatter x1, waiting for transfers between devices, local(): lax.psum_scatter(entry_grads, 'head', scatter_dimension=1, tiled=True)  36.1 us
    all_gather x1, waiting for transfers between devices, local(): entry_keys = lax.all_gather(part_keys, 'head', axis=1, tiled=True)  16.4 us
    all_to_all x1, waiting for transfers between devices, local(): lax.all_to_all(packed.reshape(owners, capacity, sub_rows, row_width), 'se...  15.6 us
    reshape x2, local copies, waits for them, and re-layouts, local(): entry_grads = d_keys.reshape(entries, BLOCK, row_width)  12.8 us
    unnamed x16, local copies, waits for them, and re-layouts  12 us
  transfers between devices with their start and end apart: 5, of which 4 were waited for; matrix products, arithmetic and copies ran while one was open for 5% of the time, Pallas kernels for 0%

commit v1 on v0

v1 whole, which is shorter than its diff:
```python
import functools

import jax
import jax.numpy as jnp
from jax import lax
from jax.experimental import pallas as pl
from jax.experimental.pallas import tpu as pltpu
from jax.sharding import PartitionSpec as P

KVL = 512
BLOCK = 128
QB = 32
TOPB = 4


SCORE_SCALE = 0.07216878364870323
MASKED = -1e30

NT = (((1,), (1,)), ((), ()))


def attention_kernel(
    slot_ref,
    rel_ref,
    q_ref,
    g_ref,
    w_ref,
    kt_ref,
    dq_ref,
    dk_ref,
    wt_ref,
    q_rows,
    dl_rows,
    lo_rows,
    dq_rows,
    kt_all,
    kn_all,
    dk_sum,
):
    heads, width, queries = q_ref.shape
    qblocks = queries // QB
    group = BLOCK // QB
    f32, bf16 = jnp.float32, jnp.bfloat16

    def spread(i, carry):
        lanes = pl.ds(pl.multiple_of(i * BLOCK, BLOCK), BLOCK)
        qs = [q_ref[i * group + j] for j in range(group)]
        ds = [
            lax.dot_general(
                w_ref[i * group + j], g_ref[i * group + j], NT, preferred_element_type=f32
            ).astype(bf16)
            for j in range(group)
        ]
        for g in range(qblocks):
            cut = slice(g * QB, (g + 1) * QB)
            q_rows[g, :, lanes] = jnp.concatenate([x[:, cut] for x in qs], axis=1)
            dl_rows[g, :, lanes] = jnp.concatenate([x[:, cut] for x in ds], axis=1)
        return carry

    lax.fori_loop(0, heads // group, spread, 0)
    dk_sum[...] = jnp.zeros_like(dk_sum)

    def block(g, carry):
        for t in range(TOPB):
            key_t = kt_ref[slot_ref[g * TOPB + t]]
            kt_all[:, t * BLOCK : (t + 1) * BLOCK] = key_t
            kn_all[t * BLOCK : (t + 1) * BLOCK, :] = key_t.T
        q_t = q_rows[g]
        dl_t = dl_rows[g]
        rows = q_t.shape[1]
        scores = jnp.dot(kn_all[...], q_t, preferred_element_type=f32) * SCORE_SCALE
        key_at = lax.broadcasted_iota(jnp.int32, (BLOCK, rows), 0)
        query_at = lax.rem(lax.broadcasted_iota(jnp.int32, (BLOCK, rows), 1), QB)
        ahead = key_at - query_at
        parts = []
        for t in range(TOPB):
            seen = ahead <= -rel_ref[g * TOPB + t]
            parts.append(jnp.where(seen, scores[t * BLOCK : (t + 1) * BLOCK], MASKED))
        scores = jnp.concatenate(parts, axis=0)
        top = jnp.max(scores, axis=0, keepdims=True)
        exps = jnp.exp(scores - top)
        weights = exps / jnp.sum(exps, axis=0, keepdims=True)
        low = weights.astype(bf16)
        latent = jnp.dot(kt_all[:KVL, :], low, preferred_element_type=f32).astype(bf16)
        lo_rows[g] = latent
        delta = jnp.sum(dl_t.astype(f32) * latent.astype(f32), axis=0, keepdims=True)
        d_probs = jnp.dot(kn_all[:, :KVL], dl_t, preferred_element_type=f32)
        d_scores = (SCORE_SCALE * weights * (d_probs - delta)).astype(bf16)
        dq_rows[g] = jnp.dot(kt_all[...], d_scores, preferred_element_type=f32).astype(bf16)
        d_keys = lax.dot_general(d_scores, q_t, NT, preferred_element_type=f32)
        d_values = lax.dot_general(low, dl_t, NT, preferred_element_type=f32)
        for t in range(TOPB):
            slot = slot_ref[g * TOPB + t]
            cut = slice(t * BLOCK, (t + 1) * BLOCK)
            dk_sum[slot, :, :KVL] += d_keys[cut, :KVL] + d_values[cut]
            dk_sum[slot, :, KVL:] += d_keys[cut, KVL:]
        return carry

    lax.fori_loop(0, qblocks, block, 0)
    dk_ref[...] = dk_sum[...].astype(dk_ref.dtype)

    def gather(i, carry):
        lanes = pl.ds(pl.multiple_of(i * BLOCK, BLOCK), BLOCK)
        qs = [dq_rows[g, :, lanes] for g in range(qblocks)]
        ls = [lo_rows[g, :, lanes] for g in range(qblocks)]
        for j in range(group):
            cut = slice(j * QB, (j + 1) * QB)
            dq_ref[i * group + j] = jnp.concatenate([x[:, cut] for x in qs], axis=1)
            latent = jnp.concatenate([x[:, cut] for x in ls], axis=1)
            wt_ref[i * group + j] = jnp.dot(
                latent, g_ref[i * group + j], preferred_element_type=f32
            ).astype(wt_ref.dtype)
        return carry

    lax.fori_loop(0, heads // group, gather, 0)


def attention(slots, rel, q_t, g_h, weight, keys_t):
    heads, width, queries = q_t.shape
    slot_total = keys_t.shape[0]
    qblocks = queries // QB
    rows = heads * QB
    macs = heads * queries * (TOPB * BLOCK * 3 * (width + KVL) + 2 * KVL * BLOCK)
    vmem = pl.BlockSpec(memory_space=pltpu.VMEM)
    smem = pl.BlockSpec(memory_space=pltpu.SMEM)
    bf16 = jnp.bfloat16
    return pl.pallas_call(
        attention_kernel,
        out_shape=(
            jax.ShapeDtypeStruct(q_t.shape, bf16),
            jax.ShapeDtypeStruct((slot_total, BLOCK, width), bf16),
            jax.ShapeDtypeStruct(weight.shape, bf16),
        ),
        in_specs=[smem, smem, vmem, vmem, vmem, vmem],
        out_specs=(vmem, vmem, vmem),
        scratch_shapes=[
            pltpu.VMEM((qblocks, width, rows), bf16),
            pltpu.VMEM((qblocks, KVL, rows), bf16),
            pltpu.VMEM((qblocks, KVL, rows), bf16),
            pltpu.VMEM((qblocks, width, rows), bf16),
            pltpu.VMEM((width, TOPB * BLOCK), bf16),
            pltpu.VMEM((TOPB * BLOCK, width), bf16),
            pltpu.VMEM((slot_total, BLOCK, width), jnp.float32),
        ],
        compiler_params=pltpu.CompilerParams(vmem_limit_bytes=60 << 20),
        cost_estimate=pl.CostEstimate(
            flops=2 * macs, bytes_accessed=16 << 20, transcendentals=rows * qblocks * 512
        ),
        name="attention",
    )(slots, rel, q_t, g_h, weight, keys_t)


def local(query, cache, grad_out, value_weight, picked):
    q_dev, heads_here, row_width = query.shape
    ctx_dev = cache.shape[0]
    owners = lax.axis_size("seq")
    seq_index = lax.axis_index("seq")
    quarters = lax.axis_size("head")
    quarter = lax.axis_index("head")
    block_count = ctx_dev // BLOCK
    qblocks_here = q_dev // QB
    entries = qblocks_here * TOPB
    capacity = max(q_dev // BLOCK, entries // owners)
    slot_total = owners * capacity
    sub_rows = BLOCK // quarters
    sub_cols = row_width // quarters
    flat_pick = picked.reshape(entries)
    owner_of = flat_pick // block_count
    global_ids = jnp.arange(owners * block_count, dtype=jnp.int32)
    matches = flat_pick[:, None] == global_ids[None, :]
    wanted = jnp.any(matches, axis=0).astype(jnp.int32).reshape(owners, block_count)
    order_in = jnp.cumsum(wanted, axis=1) - 1
    slot_ids = jnp.arange(capacity, dtype=jnp.int32)
    local_ids = jnp.arange(block_count, dtype=jnp.int32)
    holding = (wanted[:, None, :] == 1) & (order_in[:, None, :] == slot_ids[None, :, None])
    present = jnp.any(holding, axis=2)
    request = jnp.where(
        present, jnp.sum(jnp.where(holding, local_ids[None, None, :], 0), axis=2), -1
    )
    entry_rank = jnp.sum(
        jnp.where(matches, order_in.reshape(owners * block_count)[None, :], 0), axis=1
    )
    entry_slot = owner_of * capacity + entry_rank
    asked_rows = lax.all_to_all(request, "seq", split_axis=0, concat_axis=0, tiled=True).reshape(
        slot_total
    )
    owner_map = (local_ids[:, None] == asked_rows[None, :]).astype(jnp.float32)
    cache_t = cache.T
    part_t = lax.dynamic_slice_in_dim(cache_t, quarter * sub_cols, sub_cols, 0)
    part_blocks = jnp.stack(
        [part_t[:, b * BLOCK : (b + 1) * BLOCK] for b in range(block_count)]
    )
    packed = jnp.zeros((slot_total, sub_cols, BLOCK), cache.dtype)
    for b in range(block_count):
        packed = jnp.where((asked_rows == b)[:, None, None], part_blocks[b][None], packed)
    fetched = lax.all_to_all(
        packed.reshape(owners, capacity, sub_cols, BLOCK),
        "seq",
        split_axis=0,
        concat_axis=0,
        tiled=True,
    )
    keys_t = lax.all_gather(
        fetched.reshape(slot_total, sub_cols, BLOCK), "head", axis=1, tiled=True
    )
    first_pos = ctx_dev * owners - q_dev * owners + seq_index * q_dev
    rel = flat_pick * BLOCK - first_pos - (jnp.arange(entries, dtype=jnp.int32) // TOPB) * QB
    d_query_t, slot_grads, weight_terms = attention(
        entry_slot,
        rel,
        jnp.transpose(query, (1, 2, 0)),
        jnp.transpose(grad_out, (1, 0, 2)),
        value_weight,
        keys_t,
    )
    flat = weight_terms.reshape(owners, -1, weight_terms.shape[2])
    swapped = lax.all_to_all(flat, "seq", split_axis=0, concat_axis=0, tiled=True)
    summed = jnp.sum(swapped.astype(jnp.float32), axis=0).astype(jnp.bfloat16)
    d_value_weight = lax.all_gather(summed, "seq", axis=0, tiled=True).reshape(value_weight.shape)
    shares = lax.psum_scatter(slot_grads, "head", scatter_dimension=1, tiled=True)
    returned = lax.all_to_all(
        shares.reshape(owners, capacity, sub_rows, row_width),
        "seq",
        split_axis=0,
        concat_axis=0,
        tiled=True,
    )
    d_cache = jnp.dot(
        owner_map,
        returned.astype(jnp.float32).reshape(slot_total, sub_rows * row_width),
        precision=lax.Precision.HIGHEST,
    ).reshape(block_count, sub_rows, row_width)
    return (jnp.transpose(d_query_t, (2, 0, 1)), d_cache, d_value_weight)


def solution(mesh):
    in_specs = (
        P("seq", "head", None),
        P("seq", None),
        P("seq", "head", None),
        P("head", None, None),
        P("seq", None),
    )
    out_specs = (P("seq", "head", None), P("seq", "head", None), P("head", None, None))
    return jax.shard_map(local, mesh=mesh, in_specs=in_specs, out_specs=out_specs, check_vma=False)
```

time: 494 us -> 210 us (0.43)
  local copies, waits for them, and re-layouts: 160 us -> 9.35 us
  blocking collectives: 180 us -> 72.6 us
  matrix products: 38.2 us -> 0.29 us
  Pallas kernels: 0 us -> 24.2 us
  starting transfers between devices: 16.4 us -> 11.1 us
    psum x1 -> x0, blocking collectives: 180 us -> none  [local(): d_value_weight = lax.psum(weight_terms, 'seq').astype(jnp.bfloat16)]
    dynamic_update_slice x16 -> x0, local copies, waits for them, and re-layouts: 102 us -> none  [local(): d_query, d_keys, latent_out = lax.map(one_block, inputs)]
    all_to_all x0 -> x2, blocking collectives: none -> 72.6 us  [the longest x1 54.1 us: local(): lax.all_to_all(flat, 'seq', split_axis=0, concat_axis=0, tiled=True)]
    dot_general x28 -> x1, matrix products: 38.2 us -> 0.29 us  [local(): jnp.dot(owner_map, returned.astype(jnp.float32).reshape(slot_total, sub_r...]
    reduce_scatter x1, waiting for transfers between devices: 36.1 us -> 0.02 us  [local(): lax.psum_scatter(slot_grads, 'head', scatter_dimension=1, tiled=True)]
    all_gather x1 -> x2, waiting for transfers between devices: 16.4 us -> 44.1 us  [the longest x1 23.2 us: local(): lax.all_gather(summed, 'seq', axis=0, tiled=True)]
    pallas_call x0 -> x1, Pallas kernels: none -> 24.2 us  [attention(): pl.pallas_call(attention_kernel, out_shape=(jax.ShapeDtypeStruct(q_t.shap...]
    reshape x5 -> x1, local copies, waits for them, and re-layouts: 15.1 us -> 0.78 us  [local(): returned.astype(jnp.float32).reshape(slot_total, sub_rows * row_width)]
  transfers between devices with their start and end apart: 5 -> 5, of which waited for: 4 -> 4; matrix products, arithmetic and copies ran while one was open for 5% -> 3% of each run, Pallas kernels for 0% -> 0%
where the time goes in v1:
time: 210 us; the launch traced here: 209 us
  waiting for transfers between devices  74.8 us (36%)
  blocking collectives  72.6 us (35%)
  Pallas kernels  24.2 us (12%)
  between operations  13.8 us (7%)
  starting transfers between devices  11.1 us (5%)
  local copies, waits for them, and re-layouts  9.35 us (4%)
  other arithmetic  2.99 us (1%)
    all_to_all x1, blocking collectives, local(): lax.all_to_all(flat, 'seq', split_axis=0, concat_axis=0, tiled=True)  54.1 us
    all_to_all x1, waiting for transfers between devices, local(): lax.all_to_all(shares.reshape(owners, capacity, sub_rows, row_width), 'se...  24.4 us
    pallas_call x1, Pallas kernels, attention(): pl.pallas_call(attention_kernel, out_shape=(jax.ShapeDtypeStruct(q_t.shap...  24.2 us
    all_gather x1, waiting for transfers between devices, local(): lax.all_gather(summed, 'seq', axis=0, tiled=True)  23.2 us
    all_gather x1, waiting for transfers between devices, local(): lax.all_gather(fetched.reshape(slot_total, sub_cols, BLOCK), 'head', axis...  20.9 us
    all_to_all x1, blocking collectives, local(): lax.all_to_all(packed.reshape(owners, capacity, sub_cols, BLOCK), 'seq',...  18.5 us
    all_to_all x1, starting transfers between devices, local(): lax.all_to_all(request, 'seq', split_axis=0, concat_axis=0, tiled=True)  7.28 us
    all_to_all x1, waiting for transfers between devices, local(): lax.all_to_all(request, 'seq', split_axis=0, concat_axis=0, tiled=True)  6.27 us
  transfers between devices with their start and end apart: 5, of which 4 were waited for; matrix products, arithmetic and copies ran while one was open for 3% of the time, Pallas kernels for 0%

profile of v1, /device:TPU:0, one launch (start us, length us, event | category | flops | bytes accessed | tf_op | source)
XLA Modules:
  0.0 209.2 jit_solution(8598399651235506623)
XLA Ops:
  7.2 0.9 reshape.113
  8.0 0.1 fusion.2
  8.2 0.1 copy.50
  8.3 0.2 reduce_window_sum.11
  8.5 0.1 copy.51
  8.6 0.7 copy.52
  9.3 7.3 %all-to-all-start = ((s32[8,1,2]{2,1,0:T(1,128)}), s32[8,1,2]{2,1,0:T(1,128)S(1)}, u32[]{:S(2)}, u32[]{:S(2)}) async-start(s32[8,1,2]{2,1,0:T(1,128)} %copy.52), calls=%async_computation | async-start | bytes 8192 | tf_op jit(solution)/shard_map/all_to_all | solution.py:184
  16.7 6.3 %all-to-all-done = s32[8,1,2]{2,1,0:T(1,128)S(1)} async-done(((s32[8,1,2]{2,1,0:T(1,128)}), s32[8,1,2]{2,1,0:T(1,128)S(1)}, u32[]{:S(2)}, u32[]{:S(2)}) %all-to-all-start) | async-done | bytes 96 | tf_op jit(solution)/shard_map/all_to_all | solution.py:184
  23.0 0.1 copy.53
  23.1 0.1 copy.54
  23.2 0.1 copy.60
  23.3 0.1 copy.58
  23.4 0.1 copy.56
  23.5 0.3 select_select_fusion
  23.7 18.5 %all_to_all.21 = bf16[8,2,144,128]{3,2,1,0:T(8,128)(2,1)} all-to-all(bf16[8,2,144,128]{3,2,1,0:T(8,128)(2,1)S(1)} %select_select_fusion), channel_id=1, replica_groups=mesh['seq'=8,'head'=4] {'seq'}, dimensions={0} | all-to-all | bytes 1179648 | tf_op jit(solution)/shard_map/all_to_all | solution.py:196
  42.3 0.9 copy.66
  43.3 0.2 select_reduce_fusion
  43.5 0.5 fusion.9
  44.0 20.9 %all-gather.3.cloned.1.call-done.kt_ref = bf16[16,576,128]{2,1,0:T(8,128)(2,1)} async-done(((bf16[16,144,128]{2,1,0:T(8,128)(2,1)}), bf16[16,576,128]{2,1,0:T(8,128)(2,1)}) %all-gather.3.cloned.1.call-update) | async-done | bytes 2359312 | tf_op jit(solution)/shard_map/all_gather | solution.py:203
  64.8 24.2 %attention.1 = (bf16[16,576,128]{2,1,0:T(8,128)(2,1)}, bf16[16,128,576]{2,1,0:T(8,128)(2,1)}, bf16[16,512,128]{2,1,0:T(8,128)(2,1)}) custom-call(s32[16]{0:T(128)} %get-tuple-element.33.slot_ref, s32[16]{0:T(128)} %get-tuple-element.32.rel_ref, bf16[16,576,128]{2,1,0:T(8,128)(2,1)} %bitcast.35, bf16[16,128,128]{2,1,0:T(8,128)(2,1)} %bitcast.34, ...), custom_call_target="tpu_custom_call" | custom-call | flops 7381975040 | bytes 16777216 | tf_op jit(solution)/shard_map/attention/pallas_call | solution.py:127
  89.1 54.1 %all_to_all.22 = bf16[8,1024,128]{2,1,0:T(8,128)(2,1)S(1)} all-to-all(bf16[8,1024,128]{2,1,0:T(8,128)(2,1)} %bitcast.32), channel_id=1, replica_groups=mesh['seq'=8,'head'=4] {'seq'}, dimensions={0} | all-to-all | bytes 4194304 | tf_op jit(solution)/shard_map/all_to_all | solution.py:217
  143.3 1.0 reduce_sum.32
  144.3 3.7 %all-to-all-start.2 = ((bf16[8,2,32,576]{3,2,1,0:T(8,128)(2,1)}), bf16[8,2,32,576]{3,2,1,0:T(8,128)(2,1)S(1)}, u32[]{:S(2)}, u32[]{:S(2)}) async-start(bf16[8,2,32,576]{3,2,1,0:T(8,128)(2,1)} %bitcast.33), calls=%async_computation.3 | async-start | bytes 1310720 | tf_op jit(solution)/shard_map/all_to_all | solution.py:221
  148.0 0.5 broadcast.119
  148.5 0.7 reduce.4
  149.3 24.4 %all-to-all-done.2 = bf16[8,2,32,576]{3,2,1,0:T(8,128)(2,1)S(1)} async-done(((bf16[8,2,32,576]{3,2,1,0:T(8,128)(2,1)}), bf16[8,2,32,576]{3,2,1,0:T(8,128)(2,1)S(1)}, u32[]{:S(2)}, u32[]{:S(2)}) %all-to-all-start.2) | async-done | bytes 589856 | tf_op jit(solution)/shard_map/all_to_all | solution.py:221
  173.7 0.8 reshape.116
  174.5 0.8 dot_general.8
  175.3 0.3 fusion
  175.6 0.7 copy.62
  176.3 23.2 %all-gather.5.cloned.1.call-done = bf16[8192,128]{1,0:T(8,128)(2,1)} async-done(((bf16[1024,128]{1,0:T(8,128)(2,1)}), bf16[8192,128]{1,0:T(8,128)(2,1)}) %all-gather.5.cloned.1.call-update) | async-done | bytes 2097168 | tf_op jit(solution)/shard_map/all_gather | solution.py:219
  199.5 3.1 %copy.68 = bf16[16,512,128]{2,1,0:T(8,128)(2,1)} copy(bf16[16,512,128]{2,1,0:T(8,128)(2,1)} %bitcast.31) | data formatting | bytes 4194304
  (23 shorter events, 0.6 us)
Async XLA Ops:
  7.2 9.5 %copy-start = (bf16[512,576]{0,1:T(8,128)(2,1)S(1)}, bf16[512,576]{0,1:T(8,128)(2,1)}, u32[]{:S(2)}) copy-start(bf16[512,576]{0,1:T(8,128)(2,1)} %param.6) | copy-start | bytes 1769476
  7.2 35.2 %copy-start.1 = (bf16[128,16,128]{2,1,0:T(8,128)(2,1)S(1)}, bf16[128,16,128]{2,1,0:T(8,128)(2,1)}, u32[]{:S(2)}) copy-start(bf16[128,16,128]{2,1,0:T(8,128)(2,1)} %param.7) | copy-start | bytes 1572868
  9.3 13.7 %all-to-all-start = ((s32[8,1,2]{2,1,0:T(1,128)}), s32[8,1,2]{2,1,0:T(1,128)S(1)}, u32[]{:S(2)}, u32[]{:S(2)}) async-start(s32[8,1,2]{2,1,0:T(1,128)} %copy.52), calls=%async_computation | async-start | bytes 8192 | tf_op jit(solution)/shard_map/all_to_all | solution.py:184
  16.6 48.3 %all-gather.3.cloned.1.call-start = ((), (), s32[]{:S(2)}) async-start(), calls=%async_computation.5 | async-start | bytes 2949120 | tf_op jit(solution)/shard_map/all_gather | solution.py:203
  42.2 102.1 %reduce-scatter.2.cloned.1.call-start = ((), (), s32[]{:S(2)}) async-start(), calls=%async_computation.6 | async-start | bytes 3276800 | tf_op jit(solution)/shard_map/reduce_scatter | solution.py:220
  89.1 110.5 %all-gather.5.cloned.1.call-start = ((), (), s32[]{:S(2)}) async-start(), calls=%async_computation.7 | async-start | bytes 2359296 | tf_op jit(solution)/shard_map/all_gather | solution.py:219
  144.3 29.3 %all-to-all-start.2 = ((bf16[8,2,32,576]{3,2,1,0:T(8,128)(2,1)}), bf16[8,2,32,576]{3,2,1,0:T(8,128)(2,1)S(1)}, u32[]{:S(2)}, u32[]{:S(2)}) async-start(bf16[8,2,32,576]{3,2,1,0:T(8,128)(2,1)} %bitcast.33), calls=%async_computation.3 | async-start | bytes 1310720 | tf_op jit(solution)/shard_map/all_to_all | solution.py:221
Sparse Core Ops, SparseCore 0:
  42.3 22.4 all-gather.2
  89.2 34.6 reduce-scatter.1
  144.4 55.0 all-gather.4

commit v2 on v1

--- a/solution.py
+++ b/solution.py
@@ -150,6 +150,236 @@
     )(slots, rel, q_t, g_h, weight, keys_t)
 
 
+PIECES = 4
+
+
+def reduce_kernel(
+    owners,
+    quarters,
+    w_ref,
+    dk_ref,
+    out_ref,
+    ret_ref,
+    y_buf,
+    z_send,
+    z_buf,
+    mine,
+    kept,
+    half_buf,
+    final,
+    y_sem,
+    z_sem,
+    gz_sem,
+    gy_sem,
+    half_sem,
+    ret_sem,
+):
+    f32, bf16 = jnp.float32, jnp.bfloat16
+    s = lax.axis_index("seq")
+    h = lax.axis_index("head")
+    outer = owners // 2
+    a, b = s // 2, lax.rem(s, 2)
+    pair = a * 2 + 1 - b
+    cap = ret_ref.shape[1]
+    sub = ret_ref.shape[2]
+    rows = w_ref.shape[1] // PIECES
+    bits = []
+    while (1 << len(bits)) < quarters:
+        bits.append(1 << len(bits))
+
+    def flipped(bit):
+        return h + bit * (1 - 2 * lax.rem(h // bit, 2))
+
+    barrier = pltpu.get_barrier_semaphore()
+    for k in range(owners - 1):
+        pl.semaphore_signal(
+            barrier,
+            inc=1,
+            device_id=(lax.rem(s + k + 1, owners), h),
+            device_id_type=pl.DeviceIdType.MESH,
+        )
+    for bit in bits:
+        pl.semaphore_signal(
+            barrier, inc=1, device_id=(s, flipped(bit)), device_id_type=pl.DeviceIdType.MESH
+        )
+    pl.semaphore_wait(barrier, owners - 1 + len(bits))
+
+    def send(src, dst, sems, index, target):
+        copy = pltpu.make_async_remote_copy(
+            src_ref=src,
+            dst_ref=dst,
+            send_sem=sems.at[(0,) + index],
+            recv_sem=sems.at[(1,) + index],
+            device_id=target,
+            device_id_type=pl.DeviceIdType.MESH,
+        )
+        copy.start()
+        return copy
+
+    def ahead(k):
+        return lax.rem(a + k + 1, outer)
+
+    def behind(k):
+        return lax.rem(a + outer - k - 1, outer)
+
+    def owner(k):
+        return lax.rem(s + k + 1, owners)
+
+    cuts = [pl.ds(p * rows, rows) for p in range(PIECES)]
+    y_copy, z_copy, gz_copy, gy_copy = {}, {}, {}, {}
+    half_copy, ret_copy = {}, {}
+
+    first = bits[0]
+    low = lax.rem(h, 2)
+    for k in range(outer):
+        y_copy[0, k] = send(
+            w_ref.at[ahead(k) * 2 + 1 - b, cuts[0]], y_buf.at[0, k], y_sem, (0, k), (pair, h)
+        )
+    for k in range(owners):
+        slots = pl.ds(owner(k) * cap, cap)
+        for i in range(quarters // 2):
+            q = 2 * i + 1 - low
+            half_copy[0, k, i] = send(
+                dk_ref.at[slots, pl.ds(pl.multiple_of(q * sub, sub), sub)],
+                half_buf.at[0, k, i],
+                half_sem,
+                (0, k, i),
+                (s, flipped(first)),
+            )
+    for p in range(1, PIECES):
+        for k in range(outer):
+            y_copy[p, k] = send(
+                w_ref.at[ahead(k) * 2 + 1 - b, cuts[p]], y_buf.at[p, k], y_sem, (p, k), (pair, h)
+            )
+
+    def halve(level, k):
+        bit = bits[level]
+        count = quarters // (2 * bit)
+        for i in range(count):
+            half_copy[level, k, i].wait_recv()
+            if level == 0:
+                q = 2 * i + low
+                here = dk_ref[
+                    pl.ds(owner(k) * cap, cap), pl.ds(pl.multiple_of(q * sub, sub), sub)
+                ].astype(f32)
+            else:
+                here = kept[level - 1, k, 2 * i + lax.rem(h // bit, 2)].astype(f32)
+            here = here + half_buf[level, k, i].astype(f32)
+            if level + 1 < len(bits):
+                kept[level, k, i] = here.astype(bf16)
+        if level + 1 < len(bits):
+            after = bits[level + 1]
+            for i in range(count // 2):
+                other = 2 * i + 1 - lax.rem(h // after, 2)
+                half_copy[level + 1, k, i] = send(
+                    kept.at[level, k, other],
+                    half_buf.at[level + 1, k, i],
+                    half_sem,
+                    (level + 1, k, i),
+                    (s, flipped(after)),
+                )
+        elif k < owners - 1:
+            final[k] = here.astype(bf16)
+            ret_copy[k] = send(final.at[k], ret_ref.at[s], ret_sem, (k,), (owner(k), h))
+        else:
+            ret_ref[s] = here.astype(bf16)
+
+    def paired(p):
+        for k in range(outer):
+            y_copy[p, k].wait_recv()
+            part = w_ref[ahead(k) * 2 + b, cuts[p]].astype(f32) + y_buf[p, k].astype(f32)
+            if k < outer - 1:
+                z_send[p, k] = part.astype(bf16)
+                z_copy[p, k] = send(
+                    z_send.at[p, k], z_buf.at[p, k], z_sem, (p, k), (ahead(k) * 2 + b, h)
+                )
+            else:
+                mine[p] = part
+
+    def totalled(p):
+        total = mine[p]
+        for k in range(outer - 1):
+            z_copy[p, k].wait_recv()
+            total = total + z_buf[p, k].astype(f32)
+        out_ref[s, cuts[p]] = total.astype(bf16)
+        spot = out_ref.at[s, cuts[p]]
+        for k in range(outer - 1):
+            gz_copy[p, k] = send(spot, spot, gz_sem, (p, k), (ahead(k) * 2 + b, h))
+        gy_copy[p, outer - 1] = send(spot, spot, gy_sem, (p, outer - 1), (pair, h))
+
+    def forwarded(p):
+        for k in range(outer - 1):
+            gz_copy[p, k].wait_recv()
+            spot = out_ref.at[behind(k) * 2 + b, cuts[p]]
+            gy_copy[p, k] = send(spot, spot, gy_sem, (p, k), (pair, h))
+
+    for level in range(len(bits) - 1):
+        for k in range(owners):
+            halve(level, k)
+    share = -(-owners // PIECES)
+    for p in range(PIECES):
+        paired(p)
+        for k in range(p * share, min(owners, (p + 1) * share)):
+            halve(len(bits) - 1, k)
+        if p >= 1:
+            totalled(p - 1)
+        if p >= 2:
+            forwarded(p - 2)
+    totalled(PIECES - 1)
+    for p in range(max(0, PIECES - 2), PIECES):
+        forwarded(p)
+    for copy in gy_copy.values():
+        copy.wait_recv()
+    for copy in ret_copy.values():
+        copy.wait_recv()
+    for group in (y_copy, z_copy, gz_copy, gy_copy, half_copy, ret_copy):
+        for copy in group.values():
+            copy.wait_send()
+
+
+def reduce_all(owners, quarters, weight_terms, slot_grads):
+    _, rows, lanes = weight_terms.shape
+    slot_total, block, width = slot_grads.shape
+    cap = slot_total // owners
+    sub = block // quarters
+    outer = owners // 2
+    levels = max(1, quarters.bit_length() - 1)
+    piece = rows // PIECES
+    vmem = pl.BlockSpec(memory_space=pltpu.VMEM)
+    bf16, f32 = jnp.bfloat16, jnp.float32
+    dma = pltpu.SemaphoreType.DMA
+    half = quarters // 2
+    return pl.pallas_call(
+        functools.partial(reduce_kernel, owners, quarters),
+        out_shape=(
+            jax.ShapeDtypeStruct(weight_terms.shape, bf16),
+            jax.ShapeDtypeStruct((owners, cap, sub, width), bf16),
+        ),
+        in_specs=[vmem, vmem],
+        out_specs=(vmem, vmem),
+        scratch_shapes=[
+            pltpu.VMEM((PIECES, outer, piece, lanes), bf16),
+            pltpu.VMEM((PIECES, outer, piece, lanes), bf16),
+            pltpu.VMEM((PIECES, outer, piece, lanes), bf16),
+            pltpu.VMEM((PIECES, piece, lanes), f32),
+            pltpu.VMEM((levels, owners, half, cap, sub, width), bf16),
+            pltpu.VMEM((levels, owners, half, cap, sub, width), bf16),
+            pltpu.VMEM((owners, cap, sub, width), bf16),
+            dma((2, PIECES, outer)),
+            dma((2, PIECES, outer)),
+            dma((2, PIECES, outer)),
+            dma((2, PIECES, outer)),
+            dma((2, levels, owners, half)),
+            dma((2, owners)),
+        ],
+        compiler_params=pltpu.CompilerParams(
+            collective_id=0, has_side_effects=True, vmem_limit_bytes=60 << 20
+        ),
+        cost_estimate=pl.CostEstimate(flops=1 << 24, bytes_accessed=16 << 20, transcendentals=0),
+        name="reduce_all",
+    )(weight_terms, slot_grads)
+
+
 def local(query, cache, grad_out, value_weight, picked):
     q_dev, heads_here, row_width = query.shape
     ctx_dev = cache.shape[0]
@@ -213,18 +443,13 @@
         value_weight,
         keys_t,
     )
-    flat = weight_terms.reshape(owners, -1, weight_terms.shape[2])
-    swapped = lax.all_to_all(flat, "seq", split_axis=0, concat_axis=0, tiled=True)
-    summed = jnp.sum(swapped.astype(jnp.float32), axis=0).astype(jnp.bfloat16)
-    d_value_weight = lax.all_gather(summed, "seq", axis=0, tiled=True).reshape(value_weight.shape)
-    shares = lax.psum_scatter(slot_grads, "head", scatter_dimension=1, tiled=True)
-    returned = lax.all_to_all(
-        shares.reshape(owners, capacity, sub_rows, row_width),
-        "seq",
-        split_axis=0,
-        concat_axis=0,
-        tiled=True,
-    )
+    d_value_weight, returned = reduce_all(
+        owners,
+        quarters,
+        weight_terms.reshape(owners, -1, weight_terms.shape[2]),
+        slot_grads,
+    )
+    d_value_weight = d_value_weight.reshape(value_weight.shape)
     d_cache = jnp.dot(
         owner_map,
         returned.astype(jnp.float32).reshape(slot_total, sub_rows * row_width),

time: 210 us -> 182 us (0.87)
  Pallas kernels: 24.2 us -> 103 us
  blocking collectives: 72.6 us -> 18.5 us
  waiting for transfers between devices: 74.8 us -> 25.9 us
  starting transfers between devices: 11.1 us -> 7.32 us
    pallas_call x0 -> x1, Pallas kernels: none -> 78.7 us  [reduce_all(): pl.pallas_call(functools.partial(reduce_kernel, owners, quarters), out_sh...]
    all_to_all x1 -> x0, blocking collectives: 54.1 us -> none  [local(): lax.all_to_all(flat, 'seq', split_axis=0, concat_axis=0, tiled=True)]
    all_to_all x1 -> x0, waiting for transfers between devices: 24.4 us -> none  [local(): lax.all_to_all(shares.reshape(owners, capacity, sub_rows, row_width), 'se...]
    all_gather x1 -> x0, waiting for transfers between devices: 23.2 us -> none  [local(): lax.all_gather(summed, 'seq', axis=0, tiled=True)]
    all_to_all x1 -> x0, starting transfers between devices: 3.67 us -> none  [local(): lax.all_to_all(shares.reshape(owners, capacity, sub_rows, row_width), 'se...]
  transfers between devices with their start and end apart: 5 -> 2, of which waited for: 4 -> 2; matrix products, arithmetic and copies ran while one was open for 3% -> 2% of each run, Pallas kernels for 0% -> 0%
where the time goes in v2:
time: 182 us; the launch traced here: 181 us
  Pallas kernels  103 us (57%)
  waiting for transfers between devices  25.9 us (14%)
  blocking collectives  18.5 us (10%)
  between operations  14.1 us (8%)
  local copies, waits for them, and re-layouts  10.4 us (6%)
  starting transfers between devices  7.32 us (4%)
  other arithmetic  1.95 us (1%)
    pallas_call x1, Pallas kernels, reduce_all(): pl.pallas_call(functools.partial(reduce_kernel, owners, quarters), out_sh...  78.7 us
    pallas_call x1, Pallas kernels, attention(): pl.pallas_call(attention_kernel, out_shape=(jax.ShapeDtypeStruct(q_t.shap...  24.2 us
    all_gather x1, waiting for transfers between devices, local(): lax.all_gather(fetched.reshape(slot_total, sub_cols, BLOCK), 'head', axis...  19.6 us
    all_to_all x1, blocking collectives, local(): lax.all_to_all(packed.reshape(owners, capacity, sub_cols, BLOCK), 'seq',...  18.5 us
    all_to_all x1, starting transfers between devices, local(): lax.all_to_all(request, 'seq', split_axis=0, concat_axis=0, tiled=True)  7.28 us
    all_to_all x1, waiting for transfers between devices, local(): lax.all_to_all(request, 'seq', split_axis=0, concat_axis=0, tiled=True)  6.27 us
    unnamed x7, local copies, waits for them, and re-layouts  4.82 us
  transfers between devices with their start and end apart: 2, of which 2 were waited for; matrix products, arithmetic and copies ran while one was open for 2% of the time, Pallas kernels for 0%

profile of v2, /device:TPU:0, one launch (start us, length us, event | category | flops | bytes accessed | tf_op | source)
XLA Modules:
  0.0 181.4 jit_solution(18271846754589351372)
XLA Ops:
  7.2 0.9 reshape.110
  8.0 0.1 fusion.2
  8.1 0.1 reshape.115
  8.2 0.1 copy.50
  8.3 0.2 reduce_window_sum.11
  8.5 0.1 copy.51
  8.6 0.7 copy.52
  9.3 7.3 %all-to-all-start = ((s32[8,1,2]{2,1,0:T(1,128)}), s32[8,1,2]{2,1,0:T(1,128)S(1)}, u32[]{:S(2)}, u32[]{:S(2)}) async-start(s32[8,1,2]{2,1,0:T(1,128)} %copy.52), calls=%async_computation | async-start | bytes 8192 | tf_op jit(solution)/shard_map/all_to_all | solution.py:414
  16.6 0.0 all-gather.2.cloned.1.call-start
  16.7 6.3 %all-to-all-done = s32[8,1,2]{2,1,0:T(1,128)S(1)} async-done(((s32[8,1,2]{2,1,0:T(1,128)}), s32[8,1,2]{2,1,0:T(1,128)S(1)}, u32[]{:S(2)}, u32[]{:S(2)}) %all-to-all-start) | async-done | bytes 96 | tf_op jit(solution)/shard_map/all_to_all | solution.py:414
  23.0 0.1 copy.53
  23.1 0.1 copy.54
  23.2 0.1 copy.60
  23.3 0.1 copy.58
  23.4 0.1 copy.56
  23.5 0.3 select_select_fusion
  23.7 18.5 %all_to_all.11 = bf16[8,2,144,128]{3,2,1,0:T(8,128)(2,1)} all-to-all(bf16[8,2,144,128]{3,2,1,0:T(8,128)(2,1)S(1)} %select_select_fusion), channel_id=1, replica_groups=mesh['seq'=8,'head'=4] {'seq'}, dimensions={0} | all-to-all | bytes 1179648 | tf_op jit(solution)/shard_map/all_to_all | solution.py:426
  42.2 0.1 sub.24
  42.3 0.9 copy.66
  43.2 0.2 select_reduce_fusion
  43.4 0.5 fusion.9
  43.9 0.5 broadcast.119
  44.5 0.7 reduce.3
  45.1 0.1 eq.109
  45.2 19.6 %all-gather.2.cloned.1.call-done.kt_ref = bf16[16,576,128]{2,1,0:T(8,128)(2,1)} async-done(((bf16[16,144,128]{2,1,0:T(8,128)(2,1)}), bf16[16,576,128]{2,1,0:T(8,128)(2,1)}) %all-gather.2.cloned.1.call-update) | async-done | bytes 2359312 | tf_op jit(solution)/shard_map/all_gather | solution.py:433
  64.8 24.2 %attention.1 = (bf16[16,576,128]{2,1,0:T(8,128)(2,1)}, bf16[16,128,576]{2,1,0:T(8,128)(2,1)}, bf16[16,512,128]{2,1,0:T(8,128)(2,1)}) custom-call(s32[16]{0:T(128)} %get-tuple-element.37.slot_ref, s32[16]{0:T(128)} %get-tuple-element.36.rel_ref, bf16[16,576,128]{2,1,0:T(8,128)(2,1)} %bitcast.33, bf16[16,128,128]{2,1,0:T(8,128)(2,1)} %bitcast.32, ...), custom_call_target="tpu_custom_call" | custom-call | flops 7381975040 | bytes 16777216 | tf_op jit(solution)/shard_map/attention/pallas_call | solution.py:127
  89.1 78.7 %reduce_all.1 = (bf16[8,1024,128]{2,1,0:T(8,128)(2,1)}, bf16[8,2,32,576]{3,2,1,0:T(8,128)(2,1)}) custom-call(bf16[8,1024,128]{2,1,0:T(8,128)(2,1)} %bitcast.31, bf16[16,128,576]{2,1,0:T(8,128)(2,1)} %get-tuple-element.10.dk_ref), custom_call_target="tpu_custom_call" | custom-call | flops 16777216 | bytes 16777216 | tf_op jit(solution)/shard_map/reduce_all/pallas_call | solution.py:352
  167.7 1.9 %reshape.113 = bf16[16,18432]{1,0:T(8,128)(2,1)S(1)} reshape(bf16[8,2,32,576]{3,2,1,0:T(8,128)(2,1)} %get-tuple-element.11) | data formatting | bytes 1179648 | tf_op jit(solution)/shard_map/reshape | solution.py:455
  169.6 0.8 dot_general.8
  170.4 0.3 fusion
  170.7 0.7 copy.62
  171.4 3.1 %copy.68 = bf16[16,512,128]{2,1,0:T(8,128)(2,1)} copy(bf16[16,512,128]{2,1,0:T(8,128)(2,1)} %bitcast.30) | data formatting | bytes 4194304
  (14 shorter events, 0.2 us)
Async XLA Ops:
  7.2 9.5 %copy-start = (bf16[512,576]{0,1:T(8,128)(2,1)S(1)}, bf16[512,576]{0,1:T(8,128)(2,1)}, u32[]{:S(2)}) copy-start(bf16[512,576]{0,1:T(8,128)(2,1)} %param.6) | copy-start | bytes 1769476
  7.2 35.1 %copy-start.1 = (bf16[128,16,128]{2,1,0:T(8,128)(2,1)S(1)}, bf16[128,16,128]{2,1,0:T(8,128)(2,1)}, u32[]{:S(2)}) copy-start(bf16[128,16,128]{2,1,0:T(8,128)(2,1)} %param.7) | copy-start | bytes 1572868
  9.3 13.7 %all-to-all-start = ((s32[8,1,2]{2,1,0:T(1,128)}), s32[8,1,2]{2,1,0:T(1,128)S(1)}, u32[]{:S(2)}, u32[]{:S(2)}) async-start(s32[8,1,2]{2,1,0:T(1,128)} %copy.52), calls=%async_computation | async-start | bytes 8192 | tf_op jit(solution)/shard_map/all_to_all | solution.py:414
  16.6 48.3 %all-gather.2.cloned.1.call-start = ((), (), s32[]{:S(2)}) async-start(), calls=%async_computation.2 | async-start | bytes 2949120 | tf_op jit(solution)/shard_map/all_gather | solution.py:433
Sparse Core Ops, SparseCore 0:
  42.3 22.4 all-gather.1

commit v3 on v2

--- a/solution.py
+++ b/solution.py
@@ -380,20 +380,157 @@
     )(weight_terms, slot_grads)
 
 
+def fetch_kernel(
+    owners, quarters, req_ref, cache_ref, keys_ref, asked_ref, packed, req_sem, get_sem, pass_sem
+):
+    f32, bf16 = jnp.float32, jnp.bfloat16
+    s = lax.axis_index("seq")
+    h = lax.axis_index("head")
+    cap = packed.shape[1]
+    sub = packed.shape[2]
+    block_count = cache_ref.shape[1] // BLOCK
+    bits = []
+    while (1 << len(bits)) < quarters:
+        bits.insert(0, 1 << len(bits))
+
+    def flip(q, bit):
+        return q + bit * (1 - 2 * lax.rem(q // bit, 2))
+
+    def held(j):
+        q = h
+        for level, bit in enumerate(bits):
+            if (j >> level) % 2:
+                q = flip(q, bit)
+        return q
+
+    def owner(k):
+        return lax.rem(s + k + 1, owners)
+
+    def asker(k):
+        return lax.rem(s + owners - k - 1, owners)
+
+    def rows(q):
+        return pl.ds(pl.multiple_of(q * sub, sub), sub)
+
+    barrier = pltpu.get_barrier_semaphore()
+    for k in range(owners - 1):
+        pl.semaphore_signal(
+            barrier, inc=1, device_id=(owner(k), h), device_id_type=pl.DeviceIdType.MESH
+        )
+    for bit in bits:
+        pl.semaphore_signal(
+            barrier, inc=1, device_id=(s, flip(h, bit)), device_id_type=pl.DeviceIdType.MESH
+        )
+    pl.semaphore_wait(barrier, owners - 1 + len(bits))
+
+    def send(src, dst, sems, index, target):
+        copy = pltpu.make_async_remote_copy(
+            src_ref=src,
+            dst_ref=dst,
+            send_sem=sems.at[(0,) + index],
+            recv_sem=sems.at[(1,) + index],
+            device_id=target,
+            device_id_type=pl.DeviceIdType.MESH,
+        )
+        copy.start()
+        return copy
+
+    req_copy, get_copy, pass_copy = {}, {}, {}
+    for k in range(owners - 1):
+        req_copy[k] = send(
+            req_ref.at[owner(k)], asked_ref.at[s], req_sem, (k,), (owner(k), h)
+        )
+
+    def pick(ask, c):
+        chosen = jnp.zeros((sub, BLOCK), f32)
+        for b in range(block_count):
+            part = cache_ref[rows(h), b * BLOCK : (b + 1) * BLOCK].astype(f32)
+            chosen = jnp.where(ask[c : c + 1, :] == b, part, chosen)
+        return chosen.astype(bf16)
+
+    def hand_on(k, j):
+        spot = keys_ref.at[pl.ds(owner(k) * cap, cap), rows(held(j))]
+        for level in range(j.bit_length(), len(bits)):
+            index = j + (1 << level)
+            pass_copy[k, index] = send(
+                spot, spot, pass_sem, (k, index), (s, flip(h, bits[level]))
+            )
+
+    last = owners - 1
+    own = req_ref[s]
+    asked_ref[s] = own
+    for c in range(cap):
+        keys_ref[s * cap + c, rows(h)] = pick(own, c)
+    hand_on(last, 0)
+    for k in range(owners - 1):
+        req_copy[k].wait_recv()
+        ask = asked_ref[asker(k)]
+        for c in range(cap):
+            packed[k, c] = pick(ask, c)
+        get_copy[k] = send(
+            packed.at[k],
+            keys_ref.at[pl.ds(s * cap, cap), rows(h)],
+            get_sem,
+            (k,),
+            (asker(k), h),
+        )
+    for k in range(-1, owners):
+        if 0 <= k < last:
+            get_copy[k].wait_recv()
+            hand_on(k, 0)
+        before = last if k == 0 else k - 1
+        if k >= 0:
+            for j in range(1, quarters):
+                pass_copy[before, j].wait_recv()
+                hand_on(before, j)
+    for group in (req_copy, get_copy, pass_copy):
+        for copy in group.values():
+            copy.wait_send()
+
+
+def fetch(owners, quarters, request, cache_t):
+    width = cache_t.shape[0]
+    cap = request.shape[1]
+    vmem = pl.BlockSpec(memory_space=pltpu.VMEM)
+    dma = pltpu.SemaphoreType.DMA
+    padded = -(-cap // 8) * 8
+    request = jnp.pad(request, ((0, 0), (0, padded - cap)), constant_values=-1)
+    request = jnp.broadcast_to(request[:, :, None], (owners, padded, BLOCK))
+    keys_t, asked = pl.pallas_call(
+        functools.partial(fetch_kernel, owners, quarters),
+        out_shape=(
+            jax.ShapeDtypeStruct((owners * cap, width, BLOCK), cache_t.dtype),
+            jax.ShapeDtypeStruct((owners, padded, BLOCK), jnp.int32),
+        ),
+        in_specs=[vmem, vmem],
+        out_specs=(vmem, vmem),
+        scratch_shapes=[
+            pltpu.VMEM((owners, cap, width // quarters, BLOCK), cache_t.dtype),
+            dma((2, owners)),
+            dma((2, owners)),
+            dma((2, owners, quarters)),
+        ],
+        compiler_params=pltpu.CompilerParams(
+            collective_id=1, has_side_effects=True, vmem_limit_bytes=48 << 20
+        ),
+        cost_estimate=pl.CostEstimate(flops=1 << 22, bytes_accessed=4 << 20, transcendentals=0),
+        name="fetch",
+    )(request, cache_t)
+    return keys_t, asked[:, :cap, 0].reshape(owners * cap)
+
+
 def local(query, cache, grad_out, value_weight, picked):
     q_dev, heads_here, row_width = query.shape
     ctx_dev = cache.shape[0]
     owners = lax.axis_size("seq")
     seq_index = lax.axis_index("seq")
     quarters = lax.axis_size("head")
-    quarter = lax.axis_index("head")
     block_count = ctx_dev // BLOCK
     qblocks_here = q_dev // QB
     entries = qblocks_here * TOPB
     capacity = max(q_dev // BLOCK, entries // owners)
     slot_total = owners * capacity
     sub_rows = BLOCK // quarters
-    sub_cols = row_width // quarters
     flat_pick = picked.reshape(entries)
     owner_of = flat_pick // block_count
     global_ids = jnp.arange(owners * block_count, dtype=jnp.int32)
@@ -411,28 +548,8 @@
         jnp.where(matches, order_in.reshape(owners * block_count)[None, :], 0), axis=1
     )
     entry_slot = owner_of * capacity + entry_rank
-    asked_rows = lax.all_to_all(request, "seq", split_axis=0, concat_axis=0, tiled=True).reshape(
-        slot_total
-    )
+    keys_t, asked_rows = fetch(owners, quarters, request, cache.T)
     owner_map = (local_ids[:, None] == asked_rows[None, :]).astype(jnp.float32)
-    cache_t = cache.T
-    part_t = lax.dynamic_slice_in_dim(cache_t, quarter * sub_cols, sub_cols, 0)
-    part_blocks = jnp.stack(
-        [part_t[:, b * BLOCK : (b + 1) * BLOCK] for b in range(block_count)]
-    )
-    packed = jnp.zeros((slot_total, sub_cols, BLOCK), cache.dtype)
-    for b in range(block_count):
-        packed = jnp.where((asked_rows == b)[:, None, None], part_blocks[b][None], packed)
-    fetched = lax.all_to_all(
-        packed.reshape(owners, capacity, sub_cols, BLOCK),
-        "seq",
-        split_axis=0,
-        concat_axis=0,
-        tiled=True,
-    )
-    keys_t = lax.all_gather(
-        fetched.reshape(slot_total, sub_cols, BLOCK), "head", axis=1, tiled=True
-    )
     first_pos = ctx_dev * owners - q_dev * owners + seq_index * q_dev
     rel = flat_pick * BLOCK - first_pos - (jnp.arange(entries, dtype=jnp.int32) // TOPB) * QB
     d_query_t, slot_grads, weight_terms = attention(

time: 182 us -> 151 us (0.83)
  Pallas kernels: 103 us -> 138 us
  waiting for transfers between devices: 25.9 us -> 0 us
  blocking collectives: 18.5 us -> 0 us
  between operations: 14.1 us -> 0.7 us
  starting transfers between devices: 7.32 us -> 0 us
    pallas_call x0 -> x1, Pallas kernels: none -> 33.2 us  [fetch(): pl.pallas_call(functools.partial(fetch_kernel, owners, quarters), out_sha...]
    all_gather x1 -> x0, waiting for transfers between devices: 19.6 us -> none  [local(): lax.all_gather(fetched.reshape(slot_total, sub_cols, BLOCK), 'head', axis...]
    all_to_all x1 -> x0, blocking collectives: 18.5 us -> none  [local(): lax.all_to_all(packed.reshape(owners, capacity, sub_cols, BLOCK), 'seq',...]
    all_to_all x1 -> x0, starting transfers between devices: 7.28 us -> none  [local(): lax.all_to_all(request, 'seq', split_axis=0, concat_axis=0, tiled=True)]
    all_to_all x1 -> x0, waiting for transfers between devices: 6.27 us -> none  [local(): lax.all_to_all(request, 'seq', split_axis=0, concat_axis=0, tiled=True)]
    unnamed x7 -> x10, local copies, waits for them, and re-layouts: 4.82 us -> 6.62 us
  transfers between devices with their start and end apart: 2 -> 0, of which waited for: 2 -> 0; matrix products, arithmetic and copies ran while one was open for 2% -> 0% of each run, Pallas kernels for 0% -> 0%
where the time goes in v3:
time: 151 us; the launch traced here: 150 us
  Pallas kernels  138 us (91%)
  local copies, waits for them, and re-layouts  10.9 us (7%)
    pallas_call x1, Pallas kernels, reduce_all(): pl.pallas_call(functools.partial(reduce_kernel, owners, quarters), out_sh...  80.1 us
    pallas_call x1, Pallas kernels, fetch(): pl.pallas_call(functools.partial(fetch_kernel, owners, quarters), out_sha...  33.2 us
    pallas_call x1, Pallas kernels, attention(): pl.pallas_call(attention_kernel, out_shape=(jax.ShapeDtypeStruct(q_t.shap...  24.2 us
    unnamed x10, local copies, waits for them, and re-layouts  6.62 us

profile of v3, /device:TPU:0, one launch (start us, length us, event | category | flops | bytes accessed | tf_op | source)
XLA Modules:
  0.0 150.5 jit_solution(1679717670376258990)
XLA Ops:
  0.6 0.8 reshape.46
  1.4 0.1 fusion.2
  1.5 0.1 reshape.50
  1.6 0.1 copy.14
  1.7 0.2 reduce_window_sum.11
  1.8 0.1 sub.24
  1.9 0.1 copy.15
  2.0 0.2 select_reduce_fusion
  2.2 0.5 fusion.9
  2.8 0.1 copy.19
  2.9 0.1 broadcast_in_dim.44.req_ref
  2.9 2.0 %copy.23 = bf16[128,16,128]{2,0,1:T(8,128)(2,1)} copy(bf16[128,16,128]{2,1,0:T(8,128)(2,1)} %param.7) | data formatting | bytes 1048576 | tf_op args[2]
  4.9 0.0 copy-start
  4.9 1.1 copy-done
  6.0 33.2 %fetch.1 = (bf16[16,576,128]{2,1,0:T(8,128)(2,1)S(1)}, s32[8,8,128]{2,1,0:T(8,128)S(1)}) custom-call(s32[8,8,128]{2,1,0:T(8,128)S(1)} %broadcast_in_dim.44.req_ref, bf16[576,512]{1,0:T(8,128)(2,1)S(1)} %bitcast.16), custom_call_target="tpu_custom_call" | custom-call | flops 4194304 | bytes 4194304 | tf_op jit(solution)/shard_map/fetch/pallas_call | solution.py:499
  39.2 0.0 copy-start.1
  39.2 1.4 copy-done.1
  40.7 0.2 slice_reduce_fusion
  40.9 0.1 eq.61
  40.9 24.2 %attention.1 = (bf16[16,576,128]{2,1,0:T(8,128)(2,1)}, bf16[16,128,576]{2,1,0:T(8,128)(2,1)}, bf16[16,512,128]{2,1,0:T(8,128)(2,1)}) custom-call(s32[16]{0:T(128)} %get-tuple-element.27.slot_ref, s32[16]{0:T(128)} %get-tuple-element.26.rel_ref, bf16[16,576,128]{2,1,0:T(8,128)(2,1)} %bitcast.21, bf16[16,128,128]{2,1,0:T(8,128)(2,1)} %bitcast.20, ...), custom_call_target="tpu_custom_call" | custom-call | flops 7381975040 | bytes 16777216 | tf_op jit(solution)/shard_map/attention/pallas_call | solution.py:127
  65.2 80.1 %reduce_all.1 = (bf16[8,1024,128]{2,1,0:T(8,128)(2,1)}, bf16[8,2,32,576]{3,2,1,0:T(8,128)(2,1)}) custom-call(bf16[8,1024,128]{2,1,0:T(8,128)(2,1)} %bitcast.19, bf16[16,128,576]{2,1,0:T(8,128)(2,1)} %get-tuple-element.14.dk_ref), custom_call_target="tpu_custom_call" | custom-call | flops 16777216 | bytes 16777216 | tf_op jit(solution)/shard_map/reduce_all/pallas_call | solution.py:352
  145.3 0.0 copy-start.2
  145.3 2.0 %reshape.48 = bf16[16,18432]{1,0:T(8,128)(2,1)S(1)} reshape(bf16[8,2,32,576]{3,2,1,0:T(8,128)(2,1)} %get-tuple-element.15) | data formatting | bytes 1179648 | tf_op jit(solution)/shard_map/reshape | solution.py:572
  147.3 0.8 dot_general.8
  148.1 0.3 fusion
  148.4 0.7 copy.18
  149.2 0.0 copy-done.2
  149.2 1.3 copy.25
  (7 shorter events, 0.1 us)
Async XLA Ops:
  4.9 1.1 copy-start
  39.2 1.4 copy-start.1
  145.3 3.9 %copy-start.2 = (bf16[8,1024,128]{2,1,0:T(8,128)(2,1)S(1)}, bf16[8,1024,128]{2,1,0:T(8,128)(2,1)}, u32[]{:S(2)}) copy-start(bf16[8,1024,128]{2,1,0:T(8,128)(2,1)} %get-tuple-element.16) | copy-start | bytes 6291460

commit v4 on v3

--- a/solution.py
+++ b/solution.py
@@ -142,7 +142,9 @@
             pltpu.VMEM((TOPB * BLOCK, width), bf16),
             pltpu.VMEM((slot_total, BLOCK, width), jnp.float32),
         ],
-        compiler_params=pltpu.CompilerParams(vmem_limit_bytes=60 << 20),
+        compiler_params=pltpu.CompilerParams(
+            vmem_limit_bytes=(20 << 20) + slot_total * (640 << 10)
+        ),
         cost_estimate=pl.CostEstimate(
             flops=2 * macs, bytes_accessed=16 << 20, transcendentals=rows * qblocks * 512
         ),
@@ -158,7 +160,9 @@
     quarters,
     w_ref,
     dk_ref,
+    asked_ref,
     out_ref,
+    cache_ref,
     ret_ref,
     y_buf,
     z_send,
@@ -328,16 +332,23 @@
     totalled(PIECES - 1)
     for p in range(max(0, PIECES - 2), PIECES):
         forwarded(p)
+    for copy in ret_copy.values():
+        copy.wait_recv()
+    for block in range(cache_ref.shape[0]):
+        total = jnp.zeros(cache_ref.shape[1:], f32)
+        for o in range(owners):
+            for c in range(cap):
+                here = asked_ref[o, c : c + 1, 0:1] == block
+                total = total + jnp.where(here, ret_ref[o, c].astype(f32), 0.0)
+        cache_ref[block] = total
     for copy in gy_copy.values():
-        copy.wait_recv()
-    for copy in ret_copy.values():
         copy.wait_recv()
     for group in (y_copy, z_copy, gz_copy, gy_copy, half_copy, ret_copy):
         for copy in group.values():
             copy.wait_send()
 
 
-def reduce_all(owners, quarters, weight_terms, slot_grads):
+def reduce_all(owners, quarters, block_count, weight_terms, slot_grads, asked):
     _, rows, lanes = weight_terms.shape
     slot_total, block, width = slot_grads.shape
     cap = slot_total // owners
@@ -353,11 +364,12 @@
         functools.partial(reduce_kernel, owners, quarters),
         out_shape=(
             jax.ShapeDtypeStruct(weight_terms.shape, bf16),
-            jax.ShapeDtypeStruct((owners, cap, sub, width), bf16),
-        ),
-        in_specs=[vmem, vmem],
+            jax.ShapeDtypeStruct((block_count, sub, width), f32),
+        ),
+        in_specs=[vmem, vmem, vmem],
         out_specs=(vmem, vmem),
         scratch_shapes=[
+            pltpu.VMEM((owners, cap, sub, width), bf16),
             pltpu.VMEM((PIECES, outer, piece, lanes), bf16),
             pltpu.VMEM((PIECES, outer, piece, lanes), bf16),
             pltpu.VMEM((PIECES, outer, piece, lanes), bf16),
@@ -373,11 +385,13 @@
             dma((2, owners)),
         ],
         compiler_params=pltpu.CompilerParams(
-            collective_id=0, has_side_effects=True, vmem_limit_bytes=60 << 20
+            collective_id=0,
+            has_side_effects=True,
+            vmem_limit_bytes=(12 << 20) + slot_total * (750 << 10),
         ),
         cost_estimate=pl.CostEstimate(flops=1 << 24, bytes_accessed=16 << 20, transcendentals=0),
         name="reduce_all",
-    )(weight_terms, slot_grads)
+    )(weight_terms, slot_grads, asked)
 
 
 def fetch_kernel(
@@ -511,12 +525,14 @@
             dma((2, owners, quarters)),
         ],
         compiler_params=pltpu.CompilerParams(
-            collective_id=1, has_side_effects=True, vmem_limit_bytes=48 << 20
+            collective_id=1,
+            has_side_effects=True,
+            vmem_limit_bytes=(8 << 20) + owners * cap * (256 << 10),
         ),
         cost_estimate=pl.CostEstimate(flops=1 << 22, bytes_accessed=4 << 20, transcendentals=0),
         name="fetch",
     )(request, cache_t)
-    return keys_t, asked[:, :cap, 0].reshape(owners * cap)
+    return keys_t, asked
 
 
 def local(query, cache, grad_out, value_weight, picked):
@@ -548,8 +564,7 @@
         jnp.where(matches, order_in.reshape(owners * block_count)[None, :], 0), axis=1
     )
     entry_slot = owner_of * capacity + entry_rank
-    keys_t, asked_rows = fetch(owners, quarters, request, cache.T)
-    owner_map = (local_ids[:, None] == asked_rows[None, :]).astype(jnp.float32)
+    keys_t, asked = fetch(owners, quarters, request, cache.T)
     first_pos = ctx_dev * owners - q_dev * owners + seq_index * q_dev
     rel = flat_pick * BLOCK - first_pos - (jnp.arange(entries, dtype=jnp.int32) // TOPB) * QB
     d_query_t, slot_grads, weight_terms = attention(
@@ -560,18 +575,15 @@
         value_weight,
         keys_t,
     )
-    d_value_weight, returned = reduce_all(
+    d_value_weight, d_cache = reduce_all(
         owners,
         quarters,
+        block_count,
         weight_terms.reshape(owners, -1, weight_terms.shape[2]),
         slot_grads,
+        asked,
     )
     d_value_weight = d_value_weight.reshape(value_weight.shape)
-    d_cache = jnp.dot(
-        owner_map,
-        returned.astype(jnp.float32).reshape(slot_total, sub_rows * row_width),
-        precision=lax.Precision.HIGHEST,
-    ).reshape(block_count, sub_rows, row_width)
     return (jnp.transpose(d_query_t, (2, 0, 1)), d_cache, d_value_weight)
 
 

time: 151 us -> 140 us (0.927)
  Pallas kernels: 138 us -> 130 us
  local copies, waits for them, and re-layouts: 10.9 us -> 8.81 us
    pallas_call x1, Pallas kernels: 80.1 us -> 75.5 us  [reduce_all(): pl.pallas_call(functools.partial(reduce_kernel, owners, quarters), out_sh...]
    pallas_call x1, Pallas kernels: 24.2 us -> 20.9 us  [attention(): pl.pallas_call(attention_kernel, out_shape=(jax.ShapeDtypeStruct(q_t.shap...]
    reshape x1 -> x0, local copies, waits for them, and re-layouts: 2.01 us -> none  [local(): returned.astype(jnp.float32).reshape(slot_total, sub_rows * row_width)]
where the time goes in v4:
time: 140 us
  Pallas kernels  130 us (93%)
  local copies, waits for them, and re-layouts  8.81 us (6%)
    pallas_call x1, Pallas kernels, reduce_all(): pl.pallas_call(functools.partial(reduce_kernel, owners, quarters), out_sh...  75.5 us
    pallas_call x1, Pallas kernels, fetch(): pl.pallas_call(functools.partial(fetch_kernel, owners, quarters), out_sha...  33.2 us
    pallas_call x1, Pallas kernels, attention(): pl.pallas_call(attention_kernel, out_shape=(jax.ShapeDtypeStruct(q_t.shap...  20.9 us
    unnamed x10, local copies, waits for them, and re-layouts  7.62 us

profile of v4, /device:TPU:0, one launch (start us, length us, event | category | flops | bytes accessed | tf_op | source)
XLA Modules:
  0.0 139.6 jit_solution(11262512236793720273)
XLA Ops:
  0.6 0.8 reshape.40
  1.4 0.1 fusion
  1.5 0.1 reshape.43
  1.6 0.1 copy.11
  1.7 0.2 reduce_window_sum.11
  1.8 0.1 sub.24
  1.9 0.1 copy.12
  2.0 0.2 select_reduce_fusion
  2.3 0.1 copy.14
  2.4 0.1 broadcast_in_dim.43.req_ref
  2.4 1.2 copy.16
  3.6 0.0 copy-start
  3.6 1.1 copy-done
  4.7 33.2 %fetch.1 = (bf16[16,576,128]{2,1,0:T(8,128)(2,1)S(1)}, s32[8,8,128]{2,1,0:T(8,128)S(1)}) custom-call(s32[8,8,128]{2,1,0:T(8,128)S(1)} %broadcast_in_dim.43.req_ref, bf16[576,512]{1,0:T(8,128)(2,1)S(1)} %bitcast.10), custom_call_target="tpu_custom_call" | custom-call | flops 4194304 | bytes 4194304 | tf_op jit(solution)/shard_map/fetch/pallas_call | solution.py:513
  37.9 0.0 copy-start.1
  37.9 1.7 %copy-done.1 = bf16[128,16,576]{0,2,1:T(8,128)(2,1)S(1)} copy-done((bf16[128,16,576]{0,2,1:T(8,128)(2,1)S(1)}, bf16[128,16,576]{0,2,1:T(8,128)(2,1)}, u32[]{:S(2)}) %copy-start.1) | copy-done | bytes 2359320
  39.6 0.0 copy-start.2
  39.6 1.6 %copy-done.2 = bf16[16,512,128]{2,1,0:T(8,128)(2,1)S(1)} copy-done((bf16[16,512,128]{2,1,0:T(8,128)(2,1)S(1)}, bf16[16,512,128]{2,1,0:T(8,128)(2,1)}, u32[]{:S(2)}) %copy-start.2) | copy-done | bytes 2097176
  41.2 20.9 %attention.1 = (bf16[16,576,128]{2,1,0:T(8,128)(2,1)}, bf16[16,128,576]{2,1,0:T(8,128)(2,1)S(1)}, bf16[16,512,128]{2,1,0:T(8,128)(2,1)S(1)}) custom-call(s32[16]{0:T(128)S(1)} %get-tuple-element.18.slot_ref, s32[16]{0:T(128)S(1)} %get-tuple-element.17.rel_ref, bf16[16,576,128]{2,1,0:T(8,128)(2,1)S(1)} %bitcast.12, bf16[16,128,128]{2,1,0:T(8,128)(2,1)S(1)} %bitcast.11, ...), custom_call_target="tpu_custom_call" | custom-call | flops 7381975040 | bytes 16777216 | tf_op jit(solution)/shard_map/attention/pallas_call | solution.py:127
  62.1 75.5 %reduce_all.1 = (bf16[8,1024,128]{2,1,0:T(8,128)(2,1)S(1)}, f32[4,32,576]{2,1,0:T(8,128)S(1)}) custom-call(bf16[8,1024,128]{2,1,0:T(8,128)(2,1)S(1)} %bitcast.8, bf16[16,128,576]{2,1,0:T(8,128)(2,1)S(1)} %get-tuple-element.13.dk_ref, s32[8,8,128]{2,1,0:T(8,128)S(1)} %get-tuple-element.14.asked_ref), custom_call_target="tpu_custom_call" | custom-call | flops 16777216 | bytes 16777216 | tf_op jit(solution)/shard_map/reduce_all/pallas_call | solution.py:363
  137.5 0.7 copy.19
  138.3 1.3 copy.20
  (8 shorter events, 0.1 us)
Async XLA Ops:
  3.6 1.1 copy-start
  37.9 1.7 %copy-start.1 = (bf16[128,16,576]{0,2,1:T(8,128)(2,1)S(1)}, bf16[128,16,576]{0,2,1:T(8,128)(2,1)}, u32[]{:S(2)}) copy-start(bf16[128,16,576]{0,2,1:T(8,128)(2,1)} %param.5) | copy-start | bytes 7077892
  39.6 1.6 %copy-start.2 = (bf16[16,512,128]{2,1,0:T(8,128)(2,1)S(1)}, bf16[16,512,128]{2,1,0:T(8,128)(2,1)}, u32[]{:S(2)}) copy-start(bf16[16,512,128]{2,1,0:T(8,128)(2,1)} %w_ref.1) | copy-start | bytes 6291460
